TPU v7x, 128 devices: a whole 4x4x4 slice. The times are simulated.
128 devices in a mesh: rows: 8 (over y_hi, x), cols: 16 (over y_lo, z, core).
Axes of the slice: x: 4, y: 4 (y_hi: 2, y_lo: 2; y = y_hi * 2 + y_lo), z: 4, core: 2. Of those that a mesh axis runs over, the one named last changes fastest.
Arguments:
- entities: bfloat16 [16384, 4096], P('rows', 'cols'), may hold values from -20 to 20, as said below
- start_basis: float32 [4096, 512], P('cols'), may hold values from -0.09375 to 0.09375
Outputs:
- compressed: bfloat16 [16384, 512], P('rows', 'cols')
Inputs may be any that keep to these rules, and one draw needn't show every extreme that they name: `entities`: real-valued embedding entries.
All inputs are finite; a program needn't handle non-finite values.
Results may differ from a plain program's by a relative error of at most 0.0042.
Values may be sent and summed in bfloat16 or wider, within the bound.
No kernel may reach another device: no remote copies, remote signals or barrier semaphores. Data moves between devices by JAX's collectives and lax.ppermute only.
A program may use at most 128 MiB of HBM per device.

v0:
```python
import jax
import jax.numpy as jnp
from jax import lax
from jax.sharding import PartitionSpec as P

ITERS = 2


def local(entities, start_basis):
    row_count = entities.shape[0] * lax.axis_size("rows")
    gathered = lax.all_gather(entities, "cols", axis=1, tiled=True)
    cov_terms = lax.dot_general(
        entities, gathered, (((0,), (0,)), ((), ())), preferred_element_type=jnp.float32
    )
    cov_panel = lax.psum(cov_terms, "rows") / row_count
    current = start_basis
    for step in range(ITERS):
        full_basis = lax.all_gather(current, "cols", axis=0, tiled=True)
        image = jnp.dot(cov_panel, full_basis, precision=lax.Precision.HIGHEST)
        gram_term = lax.dot_general(
            image,
            image,
            (((0,), (0,)), ((), ())),
            precision=lax.Precision.HIGHEST,
            preferred_element_type=jnp.float32,
        )
        gram = lax.psum(gram_term, "cols")
        lower = jnp.linalg.cholesky(gram)
        current = jax.scipy.linalg.solve_triangular(lower, image.T, lower=True).T
    rounded = current.astype(jnp.bfloat16)
    partial_out = jnp.dot(entities, rounded, preferred_element_type=jnp.float32)
    return lax.psum_scatter(partial_out, "cols", scatter_dimension=1, tiled=True).astype(
        jnp.bfloat16
    )


def solution(mesh):
    in_specs = (P("rows", "cols"), P("cols", None))
    out_specs = P("rows", "cols")
    return jax.shard_map(local, mesh=mesh, in_specs=in_specs, out_specs=out_specs, check_vma=False)
```

profile of v0, /device:TPU:0, one launch (start us, length us, event | category | flops | bytes accessed | tf_op | source)
XLA Modules:
  0.0 962.6 jit_solution(10898096789449402941)
XLA Ops:
  8.1 102.9 %all-gather.4.cloned.1.call-done = bf16[2048,4096]{1,0:T(8,128)(2,1)} async-done(((bf16[2048,256]{1,0:T(8,128)(2,1)}), bf16[2048,4096]{1,0:T(8,128)(2,1)}) %all-gather.4.cloned.1.call-update) | async-done | bytes 16777232 | tf_op jit(solution)/shard_map/all_gather | solution.py:11
  111.0 12.7 %fusion.79 = f32[256,4096]{1,0:T(8,128)} fusion(bf16[2048,256]{1,0:T(8,128)(2,1)} %param.5, bf16[2048,4096]{1,0:T(8,128)(2,1)} %all-gather.4.cloned.1.call-done), kind=kOutput, calls=%fused_computation.144 | convolution fusion | flops 4294967296 | bytes 22020096 | tf_op jit(solution)/shard_map/dot_general | solution.py:12
  123.7 40.9 %all-gather.6.cloned.1.call-done = f32[4096,512]{1,0:T(8,128)} async-done(((f32[256,512]{1,0:T(8,128)}), f32[4096,512]{1,0:T(8,128)}) %all-gather.6.cloned.1.call-update) | async-done | bytes 8388624 | tf_op jit(solution)/shard_map/all_gather | solution.py:18
  164.6 113.3 %all-reduce.5.cloned.1.call-done = f32[256,4096]{1,0:T(8,128)} async-done(((f32[256,4096]{1,0:T(8,128)}), f32[256,4096]{1,0:T(8,128)}) %all-reduce.5.cloned.1.call-update) | async-done | bytes 4194320 | tf_op jit(solution)/shard_map/psum | solution.py:15
  277.9 10.3 %fusion.2 = f32[256,512]{1,0:T(8,128)S(1)} fusion(f32[4096,512]{1,0:T(8,128)} %all-gather.6.cloned.1.call-done, f32[256,4096]{1,0:T(8,128)} %all-reduce.5.cloned.1.call-done), kind=kOutput, calls=%fused_computation.6 | convolution fusion | flops 6443499520 | bytes 13107200 | tf_op jit(solution)/shard_map/dot_general | solution.py:19
  290.8 118.1 %all-reduce.7.cloned.1.call-done = f32[512,512]{0,1:T(8,128)} async-done(((f32[512,512]{0,1:T(8,128)}), f32[512,512]{0,1:T(8,128)}) %all-reduce.7.cloned.1.call-update) | async-done | bytes 1048592 | tf_op jit(solution)/shard_map/psum | solution.py:27
  411.9 11.7 %cholesky.286 = f32[128,128]{1,0:T(8,128)S(1)} custom-call(f32[128,128]{1,0:T(8,128)S(1)} %cholesky.426), custom_call_target="Cholesky" | custom-call | tf_op jit(solution)/shard_map/jit(cholesky)/cholesky | solution.py:28
  423.7 9.8 %custom-call.27 = f32[1,128,128]{1,2,0:T(8,128)S(1)} custom-call(f32[1,128,128]{2,1,0:T(8,128)S(1)} %get-tuple-element.62), custom_call_target="InvertDiagBlocksLowerTriangular" | custom-call | tf_op jit(solution)/shard_map/jit(cholesky)/cholesky | solution.py:28
  434.3 11.7 %cholesky.305 = f32[128,128]{1,0:T(8,128)S(1)} custom-call(f32[128,128]{1,0:T(8,128)S(1)} %cholesky.430), custom_call_target="Cholesky" | custom-call | tf_op jit(solution)/shard_map/jit(cholesky)/cholesky | solution.py:28
  446.0 10.0 %custom-call.28 = f32[1,128,128]{1,2,0:T(8,128)S(1)} custom-call(f32[1,128,128]{2,1,0:T(8,128)S(1)} %get-tuple-element.59), custom_call_target="InvertDiagBlocksLowerTriangular" | custom-call | tf_op jit(solution)/shard_map/jit(cholesky)/cholesky | solution.py:28
  456.7 11.7 %cholesky.326 = f32[128,128]{1,0:T(8,128)S(1)} custom-call(f32[128,128]{1,0:T(8,128)S(1)} %cholesky.435), custom_call_target="Cholesky" | custom-call | tf_op jit(solution)/shard_map/jit(cholesky)/cholesky | solution.py:28
  479.6 11.7 %cholesky.343 = f32[128,128]{1,0:T(8,128)S(1)} custom-call(f32[128,128]{1,0:T(8,128)S(1)} %convolution_subtract_fusion.11), custom_call_target="Cholesky" | custom-call | tf_op jit(solution)/shard_map/jit(cholesky)/cholesky | solution.py:28
  503.7 39.3 %custom-call.30 = f32[4,128,128]{1,2,0:T(8,128)S(1)} custom-call(f32[4,128,128]{2,1,0:T(8,128)S(1)} %get-tuple-element.21), custom_call_target="InvertDiagBlocksLowerTriangular" | custom-call | tf_op jit(solution)/shard_map/jit(_solve_triangular)/triangular_solve | solution.py:29
  547.0 53.2 %all-gather.8.cloned.1.call-done = f32[4096,512]{0,1:T(8,128)} async-done(((f32[256,512]{0,1:T(8,128)}), f32[4096,512]{0,1:T(8,128)}) %all-gather.8.cloned.1.call-update) | async-done | bytes 8388624 | tf_op jit(solution)/shard_map/all_gather | solution.py:18
  600.2 10.3 %fusion = f32[256,512]{1,0:T(8,128)S(1)} fusion(f32[4096,512]{0,1:T(8,128)} %all-gather.8.cloned.1.call-done, f32[256,4096]{1,0:T(8,128)} %all-reduce.5.cloned.1.call-done), kind=kOutput, calls=%fused_computation.4 | convolution fusion | flops 6443499520 | bytes 13107200 | tf_op jit(solution)/shard_map/dot_general | solution.py:19
  613.0 120.2 %all-reduce.9.cloned.1.call-done = f32[512,512]{0,1:T(8,128)} async-done(((f32[512,512]{0,1:T(8,128)}), f32[512,512]{0,1:T(8,128)}) %all-reduce.9.cloned.1.call-update) | async-done | bytes 1048592 | tf_op jit(solution)/shard_map/psum | solution.py:27
  737.3 11.7 %cholesky.358 = f32[128,128]{1,0:T(8,128)S(1)} custom-call(f32[128,128]{1,0:T(8,128)S(1)} %cholesky.439), custom_call_target="Cholesky" | custom-call | tf_op jit(solution)/shard_map/jit(cholesky)/cholesky | solution.py:28
  761.5 11.7 %cholesky.377 = f32[128,128]{1,0:T(8,128)S(1)} custom-call(f32[128,128]{1,0:T(8,128)S(1)} %cholesky.443), custom_call_target="Cholesky" | custom-call | tf_op jit(solution)/shard_map/jit(cholesky)/cholesky | solution.py:28
  774.6 10.0 %custom-call.32 = f32[1,128,128]{1,2,0:T(8,128)S(1)} custom-call(f32[1,128,128]{2,1,0:T(8,128)S(1)} %get-tuple-element.49), custom_call_target="InvertDiagBlocksLowerTriangular" | custom-call | tf_op jit(solution)/shard_map/jit(cholesky)/cholesky | solution.py:28
  786.2 11.7 %cholesky.398 = f32[128,128]{1,0:T(8,128)S(1)} custom-call(f32[128,128]{1,0:T(8,128)S(1)} %cholesky.448), custom_call_target="Cholesky" | custom-call | tf_op jit(solution)/shard_map/jit(cholesky)/cholesky | solution.py:28
  809.9 11.7 %cholesky.415 = f32[128,128]{1,0:T(8,128)S(1)} custom-call(f32[128,128]{1,0:T(8,128)S(1)} %convolution_subtract_fusion.10), custom_call_target="Cholesky" | custom-call | tf_op jit(solution)/shard_map/jit(cholesky)/cholesky | solution.py:28
  826.2 11.7 %while.5 = (s32[]{:T(128)}, f32[512,512]{1,0:T(8,128)}, s32[4,2]{0,1:T(2,128)S(1)}, f32[4,128,128]{2,1,0:T(8,128)S(1)}, s32[]{:T(128)}) while((s32[]{:T(128)}, f32[512,512]{1,0:T(8,128)}, s32[4,2]{0,1:T(2,128)S(1)}, f32[4,128,128]{2,1,0:T(8,128)S(1)}, s32[]{:T(128)}) %tuple.71), condition=%wide.while_cond.clone, body=%wide.while_body.clone.sunk | while | flops 2 | bytes 131181 | solution.py:29
  837.9 39.3 %custom-call.34 = f32[4,128,128]{1,2,0:T(8,128)S(1)} custom-call(f32[4,128,128]{2,1,0:T(8,128)S(1)} %get-tuple-element.22), custom_call_target="InvertDiagBlocksLowerTriangular" | custom-call | tf_op jit(solution)/shard_map/jit(_solve_triangular)/triangular_solve | solution.py:29
  885.7 68.1 %reduce-scatter.2.cloned.1.call-done = f32[2048,32]{0,1:T(8,128)} async-done(((f32[2048,512]{0,1:T(8,128)}), f32[2048,32]{0,1:T(8,128)}) %reduce-scatter.2.cloned.1.call-update) | async-done | bytes 262160 | tf_op jit(solution)/shard_map/reduce_scatter | solution.py:32
  (110 shorter events, 99.4 us)
Async XLA Ops:
  6.5 104.4 %all-gather.4.cloned.1.call-start = ((), (), s32[]{:S(2)}) async-start(), calls=%async_computation.1 | async-start | bytes 17825792 | tf_op jit(solution)/shard_map/all_gather | solution.py:11
  7.3 157.4 %all-gather.6.cloned.1.call-start = ((), (), s32[]{:S(2)}) async-start(), calls=%async_computation.3 | async-start | bytes 8912896 | tf_op jit(solution)/shard_map/all_gather | solution.py:18
  8.0 269.9 %all-reduce.5.cloned.1.call-start = ((), (), s32[]{:S(2)}) async-start(), calls=%async_computation.2 | async-start | bytes 8388608 | tf_op jit(solution)/shard_map/psum | solution.py:15
  123.7 285.2 %all-reduce.7.cloned.1.call-start = ((), (), s32[]{:S(2)}) async-start(), calls=%async_computation.4 | async-start | bytes 2097152 | tf_op jit(solution)/shard_map/psum | solution.py:27
  290.3 309.9 %all-gather.8.cloned.1.call-start = ((), (), s32[]{:S(2)}) async-start(), calls=%async_computation.5 | async-start | bytes 8912896 | tf_op jit(solution)/shard_map/all_gather | solution.py:18
  547.0 186.3 %all-reduce.9.cloned.1.call-start = ((), (), s32[]{:S(2)}) async-start(), calls=%async_computation.6 | async-start | bytes 2097152 | tf_op jit(solution)/shard_map/psum | solution.py:27
  612.6 341.3 %reduce-scatter.2.cloned.1.call-start = ((), (), s32[]{:S(2)}) async-start(), calls=%async_computation.7 | async-start | bytes 4456448 | tf_op jit(solution)/shard_map/reduce_scatter | solution.py:32
  736.3 1.0 copy-start.1
  784.6 98.5 %copy-start = (bf16[2048,256]{1,0:T(8,128)(2,1)S(1)}, bf16[2048,256]{1,0:T(8,128)(2,1)}, u32[]{:S(2)}) copy-start(bf16[2048,256]{1,0:T(8,128)(2,1)} %param.5) | copy-start | bytes 3145732
Sparse Core Ops, SparseCore 0:
  9.0 101.9 all-gather.3
  112.7 51.9 all-gather.5
  167.2 110.7 all-reduce.4
  290.4 118.4 all-reduce.6
  547.1 53.0 all-gather.7
  612.7 120.5 all-reduce.8
  885.9 67.9 reduce-scatter.1
where the time goes:
time: 970 us; the launch traced here: 963 us
  waiting for transfers between devices  618 us (64%)
  other arithmetic  244 us (25%)
  matrix products  56.2 us (6%)
  local copies, waits for them, and re-layouts  24.1 us (2%)
  between operations  19.2 us (2%)
    psum x2, waiting for transfers between devices, local(): gram = lax.psum(gram_term, 'cols')  238 us
    another operation x29, other arithmetic, local(): lower = jnp.linalg.cholesky(gram)  158 us
    psum x1, waiting for transfers between devices, local(): cov_panel = lax.psum(cov_terms, 'rows') / row_count  113 us
    all_gather x1, waiting for transfers between devices, local(): gathered = lax.all_gather(entities, 'cols', axis=1, tiled=True)  103 us
    all_gather x2, waiting for transfers between devices, local(): full_basis = lax.all_gather(current, 'cols', axis=0, tiled=True)  94.1 us
    another operation x5, other arithmetic, local(): current = jax.scipy.linalg.solve_triangular(lower, image.T, lower=True).T  80.3 us
    reduce_scatter x1, waiting for transfers between devices, local(): lax.psum_scatter(partial_out, 'cols', scatter_dimension=1, tiled=True)  68.1 us
    dot_general x2, matrix products, local(): image = jnp.dot(cov_panel, full_basis, precision=lax.Precision.HIGHEST)  20.5 us
  transfers between devices with their start and end apart: 7, of which 7 were waited for; matrix products, arithmetic and copies ran while one was open for 1% of the time, Pallas kernels for 0%

commit v1 on v0

v1 whole, which is shorter than its diff:
```python
import functools

import jax
import jax.numpy as jnp
from jax import lax
from jax.experimental import pallas as pl
from jax.experimental.pallas import tpu as pltpu
from jax.sharding import Mesh, PartitionSpec as P

ITERS = 2
ROWS = ("y_hi", "x")
PLANE = ("y_lo", "z")
COLS = ("y_lo", "z", "core")
HIGHEST = lax.Precision.HIGHEST
VMEM_LIMIT = 16 * 2**20
MIDDLE = 64


def full_dot(a, b, contract):
    return lax.dot_general(
        a, b, (contract, ((), ())), precision=HIGHEST, preferred_element_type=jnp.float32
    )


def spread(x):
    return jnp.broadcast_to(x, (8, 128))


def eliminate(left, right, col, row_ref):
    slot = col // 8 % 4 * 16
    row_ref[slot : slot + 8, :] = left[0]
    row_ref[slot + 8 : slot + 16, :] = right[0]
    rows_left = [row_ref[pl.ds(slot + i, 8, stride=0), :] for i in range(8)]
    rows_right = [row_ref[pl.ds(slot + 8 + i, 8, stride=0), :] for i in range(8)]
    s = [[spread(rows_left[i][:, col + j : col + j + 1]) if j >= i else None for j in range(8)] for i in range(8)]
    inverse = []
    for j in range(8):
        inverse.append(1.0 / s[j][j])
        for i in range(j + 1, 8):
            factor = s[j][i] * inverse[j]
            for k in range(i, 8):
                s[i][k] = s[i][k] - factor * s[j][k]
            rows_left[i] = rows_left[i] - factor * rows_left[j]
            rows_right[i] = rows_right[i] - factor * rows_right[j]
    row = lax.broadcasted_iota(jnp.int32, (8, 128), 0)
    done_left, done_right, scale = rows_left[0], rows_right[0], inverse[0]
    for i in range(1, 8):
        done_left = jnp.where(row == i, rows_left[i], done_left)
        done_right = jnp.where(row == i, rows_right[i], done_right)
        scale = jnp.where(row == i, inverse[i], scale)
    new_left, new_right = [], []
    for x, y in zip(left[1:], right[1:]):
        c = [spread(x[:, col + j : col + j + 1]) for j in range(8)]
        for j in range(8):
            factor = c[j] * inverse[j]
            for k in range(j + 1, 8):
                c[k] = c[k] - factor * s[j][k]
            x = x - factor * rows_left[j]
            y = y - factor * rows_right[j]
        new_left.append(x)
        new_right.append(y)
    return done_left, done_right, scale, new_left, new_right


def invert_block(a, row_ref):
    rows = lax.broadcasted_iota(jnp.int32, (128, 128), 0)
    cols = lax.broadcasted_iota(jnp.int32, (128, 128), 1)
    v = jnp.where(rows == cols, 1.0, 0.0).astype(jnp.float32)
    out = []
    for m in range(0, 128, MIDDLE):
        left = [a[i : i + 8, :] for i in range(0, MIDDLE, 8)]
        right = [v[i : i + 8, :] for i in range(0, MIDDLE, 8)]
        lefts, rights, scales = [], [], []
        for g in range(MIDDLE // 8):
            done_left, done_right, scale, left, right = eliminate(left, right, m + 8 * g, row_ref)
            lefts.append(done_left)
            rights.append(done_right)
            scales.append(scale)
        u, w, d = jnp.concatenate(lefts, 0), jnp.concatenate(rights, 0), jnp.concatenate(scales, 0)
        out.append(w * jnp.sqrt(d))
        if m + MIDDLE < 128:
            factors = (u * d)[:, m + MIDDLE :]
            a = a[MIDDLE:] - full_dot(factors, u, ((0,), (0,)))
            v = v[MIDDLE:] - full_dot(factors, w, ((0,), (0,)))
    return jnp.concatenate(out, 0)


IN_VMEM = pl.BlockSpec(memory_space=pltpu.VMEM)
IN_SMEM = pl.BlockSpec(memory_space=pltpu.SMEM)
ANYWHERE = pl.BlockSpec(memory_space=pl.ANY)


def on_chip(kernel, outputs, scratch, flops, name):
    def call(where, *operands, after=()):
        return pl.pallas_call(
            kernel,
            out_shape=outputs,
            in_specs=[IN_SMEM] + [IN_VMEM] * len(operands) + [ANYWHERE] * len(after),
            out_specs=[IN_VMEM] * len(outputs),
            scratch_shapes=scratch,
            compiler_params=pltpu.CompilerParams(vmem_limit_bytes=VMEM_LIMIT),
            cost_estimate=pl.CostEstimate(flops=flops, bytes_accessed=2**20, transcendentals=0),
            name=name,
        )(where, *operands, *after)

    return call


def pass_kernel(*refs):
    pass


def together(arrays, after):
    n = len(arrays)
    return pl.pallas_call(
        pass_kernel,
        out_shape=[jax.ShapeDtypeStruct(x.shape, x.dtype) for x in arrays],
        in_specs=[ANYWHERE] * (n + 1),
        out_specs=[ANYWHERE] * n,
        input_output_aliases={i: i for i in range(n)},
        name="together",
    )(*arrays, after)


def hold_kernel(where_ref, x_ref, out_ref, top_ref):
    out_ref[...] = x_ref[...]
    top_ref[...] = x_ref[: top_ref.shape[0], :]


def hold(where, x):
    outputs = [array(x.shape, x.dtype), array((x.shape[0] // 2, x.shape[1]), x.dtype)]
    return on_chip(hold_kernel, outputs, [], 10**9, "hold")(where, x)


def array(shape, dtype=jnp.float32):
    return jax.ShapeDtypeStruct(shape, dtype)


GRAY = (0, 1, 3, 2)


def gray(step):
    return step ^ lax.shift_right_logical(step, 1)


def behind(outer, inner, a, m):
    return (outer ^ a) * 4 + lax.rem(inner + 4 - GRAY[m], 4)


def rows_of(block, width):
    return pl.ds(pl.multiple_of(block * width, 8), width)


def load_gram(where_ref, mine_ref, other_ref, a_ref):
    core = where_ref[4]
    blocks, half = mine_ref.shape[:2]
    for i in range(blocks):
        a_ref[rows_of(2 * i + core, half), :] = mine_ref[i]
        a_ref[rows_of(2 * i + 1 - core, half), :] = other_ref[i]


def factor(w_ref, a_ref, row_ref):
    n = w_ref.shape[0]
    w_ref[...] = jnp.zeros_like(w_ref)
    for k in range(0, n, 128):
        block = slice(k, k + 128)
        w = invert_block(a_ref[block, block], row_ref)
        if k:
            w_ref[block, :k] = full_dot(w, w_ref[block, :k], ((1,), (0,)))
        w_ref[block, block] = w
        if k + 128 < n:
            u = full_dot(w, a_ref[block, k + 128 :], ((1,), (0,)))
            a_ref[k + 128 :, k + 128 :] -= full_dot(u, u, ((0,), (0,)))
            w_ref[k + 128 :, : k + 128] -= full_dot(u, w_ref[block, : k + 128], ((0,), (0,)))


def last_basis_kernel(where_ref, mine_ref, other_ref, image_ref, out_ref, w_ref, a_ref, row_ref):
    load_gram(where_ref, mine_ref, other_ref, a_ref)
    factor(w_ref, a_ref, row_ref)
    width = out_ref.shape[0]
    mine = w_ref[rows_of(where_ref[2] * 4 + where_ref[3], width), :]
    out_ref[...] = full_dot(mine, image_ref[...], ((1,), (0,))).astype(out_ref.dtype)


def last_basis(where, mine, other, image):
    n = mine.shape[2]
    square = pltpu.VMEM((n, n), jnp.float32)
    outputs = [array((2 * mine.shape[1], image.shape[1]), jnp.bfloat16)]
    scratch = [square, square, pltpu.VMEM((64, 128), jnp.float32)]
    return on_chip(last_basis_kernel, outputs, scratch, 200 * n**3, "last_basis")(where, mine, other, image)[0]


def put_in_order(where_ref, pieces, block_ref):
    width = pieces[0].shape[1]
    for m, piece in enumerate(pieces):
        for a in range(2):
            block_ref[rows_of(behind(where_ref[2], where_ref[3], a, m), width), :] = piece[a]


def gram_rows(where_ref, block_ref, part_ref, keep_ref, give_ref):
    half = keep_ref.shape[0]
    core = where_ref[4]
    mine = block_ref[rows_of(where_ref[2] * 4 + where_ref[3], 2 * half), :]
    part_ref[...] = full_dot(mine, block_ref[...], ((1,), (1,)))
    keep_ref[...] = part_ref[rows_of(core, half), :]
    give_ref[...] = part_ref[rows_of(1 - core, half), :]


def gram_kernel(where_ref, *refs):
    keep_ref, give_ref, block_ref, part_ref = refs[4:]
    put_in_order(where_ref, refs[:4], block_ref)
    gram_rows(where_ref, block_ref, part_ref, keep_ref, give_ref)


def gram_terms(where, pieces):
    width, features = pieces[0].shape[1:]
    n = 8 * width
    outputs = [array((width // 2, n))] * 2
    scratch = [pltpu.VMEM((n, features), jnp.float32), pltpu.VMEM((width, n), jnp.float32)]
    return on_chip(gram_kernel, outputs, scratch, 2 * 10**9, "gram_terms")(where, *pieces)


def add_kernel(where_ref, *refs):
    pieces, out_ref, terms_ref = refs[:4], refs[4], refs[5]
    for m, piece in enumerate(pieces):
        for a in range(2):
            terms_ref[behind(where_ref[0], where_ref[1], a, m)] = piece[a]
    total = sum(terms_ref[i] for i in range(8))
    for i in range(8):
        out_ref[i] = total


def add_in_order(where, pieces):
    outputs = [array((8,) + pieces[0].shape[1:])]
    return on_chip(add_kernel, outputs, [pltpu.VMEM(outputs[0].shape, jnp.float32)], 10**9, "add_in_order")(
        where, *pieces
    )[0]


def add_both_kernel(scale, where_ref, x_ref, out_ref):
    total = sum(x_ref[i] for i in range(8))
    width = total.shape[0] // 2
    for i in range(8):
        out_ref[i, :width] = total[:width] * scale
        out_ref[i, width:] = total[width:]


def add_both(where, x, scale):
    kernel = functools.partial(add_both_kernel, scale)
    return on_chip(kernel, [array(x.shape)], [], 10**9, "add_both")(where, x)[0]


def normalised_kernel(where_ref, mine_ref, other_ref, image_ref, keep_ref, give_ref, product_ref, w_ref, a_ref, row_ref, part_ref):
    blocks, width, features = mine_ref.shape
    width //= 2
    half = width // 2
    core = where_ref[4]
    for i in range(blocks):
        product_ref[rows_of(i, width), :] = mine_ref[i, :width]
        for j in range(2):
            at = slice(width + j * half, width + (j + 1) * half)
            columns = slice(j * features, (j + 1) * features)
            a_ref[rows_of(2 * i + core, half), columns] = mine_ref[i, at]
            a_ref[rows_of(2 * i + 1 - core, half), columns] = other_ref[i, at]
    factor(w_ref, a_ref, row_ref)
    image_ref[...] = full_dot(w_ref[...], product_ref[...], ((1,), (0,)))
    gram_rows(where_ref, image_ref, part_ref, keep_ref, give_ref)


def normalised(where, mine, other):
    _, width, features = mine.shape
    width //= 2
    n = 8 * width
    outputs = [array((n, features)), array((width // 2, n)), array((width // 2, n))]
    square = pltpu.VMEM((n, n), jnp.float32)
    scratch = [pltpu.VMEM((n, features), jnp.float32), square, square, pltpu.VMEM((64, 128), jnp.float32)]
    scratch += [pltpu.VMEM((width, n), jnp.float32)]
    return on_chip(normalised_kernel, outputs, scratch, 200 * n**3, "normalised")(where, mine, other)


PIECES = [(0, 0, 2), (1, 0, 2), (2, 0, 2), (3, 0, 2), (4, 0, 2), (5, 0, 2), (6, 0, 2), (7, 0, 1), (7, 1, 1)]
BLOCKS = 8


def three_parts(x):
    high = x.astype(jnp.bfloat16)
    rest = x - high.astype(jnp.float32)
    middle = rest.astype(jnp.bfloat16)
    low = (rest - middle.astype(jnp.float32)).astype(jnp.bfloat16)
    return jnp.concatenate([high, middle, low], 0)


def add_parts(total, width):
    return total[:width] + total[width : 2 * width] + total[2 * width :]


def weights(x):
    return (three_parts(x) if x.dtype == jnp.float32 else x).T


def multiply(pieces, weights_ref, store, rows, width):
    tile = rows // 4
    for quarter in range(4):
        total = 0.0
        for piece, (k, first, count) in zip(pieces, PIECES):
            start = quarter * tile - first * rows // 2
            if 0 <= start < count * rows // 2:
                total += jnp.dot(piece[start : start + tile, :], weights_ref[k], preferred_element_type=jnp.float32)
        total = total.T
        store(slice(quarter * tile, (quarter + 1) * tile), add_parts(total, width) if len(total) > width else total)


def first_kernel(where_ref, basis_ref, *refs):
    pieces, out_ref, weights_ref = refs[:-2], refs[-2], refs[-1]
    for a in range(2):
        for m in range(4):
            weights_ref[4 * a + m] = weights(basis_ref[behind(where_ref[2], where_ref[3], a, m)])
    width, rows = out_ref.shape

    def store(at, value):
        out_ref[:, at] = value

    multiply(pieces, weights_ref, store, rows, width)


def load_from_rows(where_ref, basis, weights_ref):
    for m in range(4):
        for a in range(2):
            block = behind(where_ref[0], where_ref[1], a, m)
            step = lax.rem(where_ref[3] + 4 - lax.rem(block, 4), 4)
            place = (lax.div(block, 4) ^ where_ref[2]) * 4 + gray(step)
            weights_ref[place] = weights(basis[m][a])


def next_kernel(where_ref, *refs):
    pieces, out_ref, weights_ref = refs[4:-2], refs[-2], refs[-1]
    load_from_rows(where_ref, refs[:4], weights_ref)
    width, rows = out_ref.shape

    def store(at, value):
        out_ref[:, at] = value

    multiply(pieces, weights_ref, store, rows, width)


def compressed_kernel(where_ref, *refs):
    pieces, (keep_ref, give_ref, weights_ref, out_ref) = refs[4:-4], refs[-4:]
    load_from_rows(where_ref, refs[:4], weights_ref)
    width, rows = out_ref.shape
    half = width // 2
    core = where_ref[4]

    def store(at, value):
        out_ref[:, at] = value

    multiply(pieces, weights_ref, store, rows, width)
    keep_ref[...] = out_ref[rows_of(core, half), :]
    give_ref[...] = out_ref[rows_of(1 - core, half), :]


def product_flops(rows, width, features):
    return 16 * rows * width * BLOCKS * features


def first_product(where, basis, pieces):
    width, features = basis.shape[1:]
    rows = pieces[0].shape[0]
    scratch = [pltpu.VMEM((BLOCKS, features, 3 * width), jnp.bfloat16)]
    return on_chip(first_kernel, [array((width, rows))], scratch, product_flops(rows, width, features), "first_product")(
        where, basis, *pieces
    )[0]


def next_product(where, basis, pieces):
    width, features = basis[0].shape[1:]
    rows = pieces[0].shape[0]
    scratch = [pltpu.VMEM((BLOCKS, features, 3 * width), jnp.bfloat16)]
    return on_chip(next_kernel, [array((width, rows))], scratch, product_flops(rows, width, features), "next_product")(
        where, *basis, *pieces
    )[0]


def compress(where, basis, pieces):
    width, features = basis[0].shape[1:]
    rows = pieces[0].shape[0]
    outputs = [array((width // 2, rows))] * 2
    scratch = [pltpu.VMEM((BLOCKS, features, width), jnp.bfloat16), pltpu.VMEM((width, rows), jnp.float32)]
    return on_chip(compressed_kernel, outputs, scratch, product_flops(rows, width, features), "compress")(
        where, *basis, *pieces
    )


def back_kernel(where_ref, mine_ref, other_ref, *refs):
    pieces, outs, (sums_ref, parts_ref) = refs[:-6], refs[-6:-2], refs[-2:]
    width, rows = mine_ref.shape
    parts_ref[...] = three_parts(mine_ref[...] + other_ref[...])
    for block in range(BLOCKS):
        total = 0.0
        for piece, (k, first, count) in zip(pieces, PIECES):
            if k == block:
                at = slice(first * rows // 2, (first + count) * rows // 2)
                total += jnp.dot(parts_ref[:, at], piece[...], preferred_element_type=jnp.float32)
        target = behind(where_ref[2], where_ref[3], block // 4, block % 4)
        step = lax.rem(lax.rem(target, 4) + 4 - where_ref[1], 4)
        sums_ref[gray(step) * 2 + (lax.div(target, 4) ^ where_ref[0])] = add_parts(total, width)
    for m in range(4):
        outs[m][...] = sums_ref[2 * m : 2 * m + 2]


def back_and_gram_kernel(where_ref, mine_ref, other_ref, keep_ref, got_ref, *refs):
    pieces, (out_ref, parts_ref) = refs[:-2], refs[-2:]
    width, rows = mine_ref.shape
    features = out_ref.shape[2]
    gram = keep_ref[...] + got_ref[...]
    half = gram.shape[0]
    for i in range(BLOCKS):
        for j in range(2):
            out_ref[i, width + j * half : width + (j + 1) * half] = gram[:, j * features : (j + 1) * features]
    parts_ref[...] = three_parts(mine_ref[...] + other_ref[...])
    for block in range(BLOCKS):
        total = 0.0
        for piece, (k, first, count) in zip(pieces, PIECES):
            if k == block:
                at = slice(first * rows // 2, (first + count) * rows // 2)
                total += jnp.dot(parts_ref[:, at], piece[...], preferred_element_type=jnp.float32)
        target = behind(where_ref[2], where_ref[3], block // 4, block % 4)
        out_ref[target, :width] = add_parts(total, width)


def back_and_gram(where, mine, other, keep, got, pieces):
    width, rows = mine.shape
    features = pieces[0].shape[1]
    outputs = [array((BLOCKS, 2 * width, features))]
    scratch = [pltpu.VMEM((3 * width, rows), jnp.bfloat16)]
    return on_chip(back_and_gram_kernel, outputs, scratch, product_flops(rows, width, features), "back_and_gram")(
        where, mine, other, keep, got, *pieces
    )[0]


def back_product(where, mine, other, pieces):
    width, rows = mine.shape
    features = pieces[0].shape[1]
    outputs = [array((2, width, features))] * 4
    scratch = [pltpu.VMEM((BLOCKS, width, features), jnp.float32), pltpu.VMEM((3 * width, rows), jnp.bfloat16)]
    return on_chip(back_kernel, outputs, scratch, product_flops(rows, width, features), "back_product")(
        where, mine, other, *pieces
    )


def exchange(x, axes):
    return lax.all_to_all(x, axes, 0, 0, tiled=True)


def swap(x, axis):
    return lax.ppermute(x, axis, [(0, 1), (1, 0)])


def shift(x, axis, step):
    return lax.ppermute(x, axis, [(i, (i + step) % 4) for i in range(4)])


def fan_out(x, axes):
    outer, inner = axes
    pair = jnp.stack([x, swap(x, outer)])
    return [pair] + [shift(pair, inner, GRAY[m]) for m in (1, 2, 3)]


def fan_in(pairs, axes):
    outer, inner = axes
    pair = pairs[0] + sum(shift(pairs[m], inner, GRAY[m]) for m in (1, 2, 3))
    return pair[0] + swap(pair[1], outer)


def gather_entities(where, x, basis):
    half = x.shape[0] // 2
    before, after = shift(x, "z", 1), shift(x, "z", 3)
    across = swap(x, "y_lo")
    before, after, across = together([before, after, across], basis)
    far = shift(before, "z", 1)
    across_before = swap(before, "y_lo")
    across_after = shift(across, "z", 3)
    far, far_half = hold(where, far)
    far_top = swap(far_half, "y_lo")
    far_low = shift(across_after[half:], "z", 3)
    return [hold(where, x)[0], before, after, far, across, across_before, across_after, far_top, far_low]


def whole_gram(where, part):
    part = exchange(add_in_order(where, fan_out(part, ROWS)), PLANE)
    return part, swap(part, "core")


def local(entities, start_basis):
    rows, features = entities.shape
    total_rows = rows * lax.axis_size(ROWS)
    width = start_basis.shape[1] // 8
    where = jnp.stack([lax.axis_index(a) for a in ROWS + COLS]).astype(jnp.int32)

    basis = exchange(start_basis.T.reshape(8, width, features), PLANE)
    pieces = gather_entities(where, entities, basis)

    image = first_product(where, basis, pieces)
    image = fan_in(back_product(where, image, swap(image, "core"), pieces), ROWS) / total_rows
    keep, give = gram_terms(where, fan_out(image, PLANE))
    for step in range(1, ITERS):
        product = next_product(where, fan_out(image, ROWS), pieces)
        sent = back_and_gram(where, product, swap(product, "core"), keep, swap(give, "core"), pieces)
        both = exchange(add_both(where, exchange(sent, ROWS), 1.0 / total_rows), PLANE)
        block, keep, give = normalised(where, both, swap(both, "core"))
    part = keep + swap(give, "core")
    rounded = last_basis(where, *whole_gram(where, part), block)
    keep, give = compress(where, fan_out(rounded, ROWS), pieces)
    return (keep + swap(give, "core")).T.astype(jnp.bfloat16)


def solution(mesh):
    fine = Mesh(mesh.devices.reshape(2, 4, 2, 4, 2), ROWS + COLS)
    return jax.shard_map(
        local,
        mesh=fine,
        in_specs=(P(ROWS, COLS), P(COLS, None)),
        out_specs=P(ROWS, COLS),
        check_vma=False,
    )
```

time: 970 us -> 282 us (0.29)
  waiting for transfers between devices: 618 us -> 82.9 us
  other arithmetic: 244 us -> 0.77 us
  blocking collectives: 0 us -> 78.8 us
  Pallas kernels: 0 us -> 67.7 us
  matrix products: 56.2 us -> 0 us
  starting transfers between devices: 1.12 us -> 42.2 us
  local copies, waits for them, and re-layouts: 24.1 us -> 4.46 us
  between operations: 19.2 us -> 0.51 us
    psum x3 -> x0, waiting for transfers between devices: 352 us -> none  [the longest x2 238 us: local(): gram = lax.psum(gram_term, 'cols')]
    another operation x34 -> x3, other arithmetic: 238 us -> 0.03 us  [fan_out(): pair = jnp.stack([x, swap(x, outer)])]
    all_gather x3 -> x0, waiting for transfers between devices: 197 us -> none  [the longest x1 103 us: local(): gathered = lax.all_gather(entities, 'cols', axis=1, tiled=True)]
    ppermute x0 -> x35, waiting for transfers between devices: none -> 82.9 us  [the longest x20 55.2 us: shift(): return lax.ppermute(x, axis, [(i, (i + step) % 4) for i in range(4)])]
    all_to_all x0 -> x4, blocking collectives: none -> 78.8 us  [exchange(): return lax.all_to_all(x, axes, 0, 0, tiled=True)]
    reduce_scatter x1 -> x0, waiting for transfers between devices: 68.1 us -> none  [local(): lax.psum_scatter(partial_out, 'cols', scatter_dimension=1, tiled=True)]
    pallas_call x0 -> x13, Pallas kernels: none -> 67.7 us  [the longest x12 67.7 us: call(): pl.pallas_call(kernel, out_shape=outputs, in_specs=[IN_SMEM] + [IN_VMEM]...]
    ppermute x0 -> x35, starting transfers between devices: none -> 42.2 us  [the longest x20 28.4 us: shift(): return lax.ppermute(x, axis, [(i, (i + step) % 4) for i in range(4)])]
  transfers between devices with their start and end apart: 7 -> 35, of which waited for: 7 -> 27; matrix products, arithmetic and copies ran while one was open for 1% -> 1% of each run, Pallas kernels for 0% -> 1%
where the time goes in v1:
time: 282 us; the launch traced here: 277 us
  waiting for transfers between devices  82.9 us (29%)
  blocking collectives  78.8 us (28%)
  Pallas kernels  67.7 us (24%)
  starting transfers between devices  42.2 us (15%)
  local copies, waits for them, and re-layouts  4.46 us (2%)
    all_to_all x4, blocking collectives, exchange(): return lax.all_to_all(x, axes, 0, 0, tiled=True)  78.8 us
    pallas_call x12, Pallas kernels, call(): pl.pallas_call(kernel, out_shape=outputs, in_specs=[IN_SMEM] + [IN_VMEM]...  67.7 us
    ppermute x20, waiting for transfers between devices, shift(): return lax.ppermute(x, axis, [(i, (i + step) % 4) for i in range(4)])  55.2 us
    ppermute x20, starting transfers between devices, shift(): return lax.ppermute(x, axis, [(i, (i + step) % 4) for i in range(4)])  28.4 us
    ppermute x15, waiting for transfers between devices, swap(): return lax.ppermute(x, axis, [(0, 1), (1, 0)])  27.7 us
    ppermute x15, starting transfers between devices, swap(): return lax.ppermute(x, axis, [(0, 1), (1, 0)])  13.8 us
  transfers between devices with their start and end apart: 35, of which 27 were waited for; matrix products, arithmetic and copies ran while one was open for 1% of the time, Pallas kernels for 1%

profile of v1, /device:TPU:0, one launch (start us, length us, event | category | flops | bytes accessed | tf_op | source)
XLA Modules:
  0.0 277.4 jit_solution(2656608118410379234)
XLA Ops:
  7.7 27.2 %all_to_all.20.refs_3_.basis_ref = f32[8,64,256]{2,1,0:T(8,128)} all-to-all(f32[8,64,256]{2,1,0:T(8,128)} %bitcast.25), channel_id=1, replica_groups=mesh['y_hi'=2,'x'=4,'y_lo'=2,'z'=4,'core'=2] {'y_lo','z'}, dimensions={0} | all-to-all | bytes 1048576 | tf_op jit(solution)/shard_map/all_to_all | solution.py:451
  40.9 19.8 %collective-permute-done.5.refs_6_.refs_10_ = bf16[2048,256]{1,0:T(8,128)(2,1)S(1)} collective-permute-done((bf16[2048,256]{1,0:T(8,128)(2,1)}, bf16[2048,256]{1,0:T(8,128)(2,1)S(1)}, u32[]{:S(2)}, u32[]{:S(2)}) %collective-permute-start.5) | collective-permute-done | bytes 1048608 | tf_op jit(solution)/shard_map/ppermute | solution.py:459
  60.8 3.1 %collective-permute-start.7 = (bf16[1024,256]{1,0:T(8,128)(2,1)S(1)}, bf16[1024,256]{1,0:T(8,128)(2,1)S(1)}, u32[]{:S(2)}, u32[]{:S(2)}) collective-permute-start(bf16[1024,256]{1,0:T(8,128)(2,1)S(1)} %slice.12), channel_id=1, source_target_pairs={{0,6},{2,0},{4,2},{6,4},{1,7},{3,1},{5,3},{7,5},{8,14},{10,8},{12,... | collective-permute-start | bytes 1572872 | tf_op jit(solution)/shard_map/ppermute | solution.py:459
  66.8 5.2 %collective-permute-done.7.refs_8_.refs_12_ = bf16[1024,256]{1,0:T(8,128)(2,1)S(1)} collective-permute-done((bf16[1024,256]{1,0:T(8,128)(2,1)S(1)}, bf16[1024,256]{1,0:T(8,128)(2,1)S(1)}, u32[]{:S(2)}, u32[]{:S(2)}) %collective-permute-start.7) | collective-permute-done | bytes 524320 | tf_op jit(solution)/shard_map/ppermute | solution.py:459
  72.0 2.7 collective-permute-done.6.refs_7_.refs_11_
  74.8 3.3 %first_product.1.mine_ref = f32[64,2048]{1,0:T(8,128)S(1)} custom-call(s32[5]{0:T(128)S(1)} %stack.57.where_ref, f32[8,64,256]{2,1,0:T(8,128)S(1)} %copy-done, bf16[2048,256]{1,0:T(8,128)(2,1)S(1)} %get-tuple-element.22.refs_0_.refs_4_, bf16[2048,256]{1,0:T(8,128)(2,1)S(1)} %copy-done.2, bf16[2048,256]{1,0:T(8,128)(2,1)S(1)} %copy-done.6, ...), custom_call_target="tpu_custom_call" | custom-call | flops 4294967296 | bytes 1048576 | tf_op jit(solution)/shard_map/first_product/pallas_call | solution.py:95
  93.1 3.2 %collective-permute-start.12 = (f32[64,256]{1,0:T(8,128)S(1)}, f32[64,256]{1,0:T(8,128)S(1)}, u32[]{:S(2)}, u32[]{:S(2)}) collective-permute-start(f32[64,256]{1,0:T(8,128)S(1)} %slice_bitcast_fusion), channel_id=1, source_target_pairs={{0,64},{64,0},{1,65},{65,1},{2,66},{66,2},{3,67},{67,3},{4,68},{68... | collective-permute-start | bytes 196616 | tf_op jit(solution)/shard_map/ppermute | solution.py:455
  96.3 2.7 collective-permute-done.12
  106.9 2.8 %collective-permute-start.15 = (f32[2,64,256]{2,1,0:T(8,128)S(1)}, f32[2,64,256]{2,1,0:T(8,128)S(1)}, u32[]{:S(2)}, u32[]{:S(2)}) collective-permute-start(f32[2,64,256]{2,1,0:T(8,128)S(1)} %get-tuple-element.40.refs_0_), channel_id=1, source_target_pairs={{0,48},{16,0},{32,16},{48,32},{1,49},{17,1},{33,17},{49,33},{2,50}... | collective-permute-start | bytes 393224 | tf_op jit(solution)/shard_map/ppermute | solution.py:459
  109.8 2.7 collective-permute-done.16.refs_3_
  113.1 2.8 %collective-permute-done.14.refs_1_ = f32[2,64,256]{2,1,0:T(8,128)S(1)} collective-permute-done((f32[2,64,256]{2,1,0:T(8,128)S(1)}, f32[2,64,256]{2,1,0:T(8,128)S(1)}, u32[]{:S(2)}, u32[]{:S(2)}) %collective-permute-start.14) | collective-permute-done | bytes 131104 | tf_op jit(solution)/shard_map/ppermute | solution.py:459
  115.9 3.4 %next_product.1.mine_ref = f32[64,2048]{1,0:T(8,128)S(1)} custom-call(s32[5]{0:T(128)S(1)} %stack.57.where_ref, f32[2,64,256]{2,1,0:T(8,128)S(1)} %get-tuple-element.40.refs_0_, f32[2,64,256]{2,1,0:T(8,128)S(1)} %collective-permute-done.14.refs_1_, f32[2,64,256]{2,1,0:T(8,128)S(1)} %collective-permute-done.15.refs_2_, ...), custom_call_target="tpu_custom_call" | custom-call | flops 4294967296 | bytes 1048576 | tf_op jit(solution)/shard_map/next_product/pallas_call | solution.py:95
  123.2 4.3 %collective-permute-done.21.refs_3_ = f32[2,64,256]{2,1,0:T(8,128)S(1)} collective-permute-done((f32[2,64,256]{2,1,0:T(8,128)S(1)}, f32[2,64,256]{2,1,0:T(8,128)S(1)}, u32[]{:S(2)}, u32[]{:S(2)}) %collective-permute-start.21) | collective-permute-done | bytes 131104 | tf_op jit(solution)/shard_map/ppermute | solution.py:459
  134.8 21.2 %all_to_all.21.x_ref = f32[8,128,256]{2,1,0:T(8,128)S(1)} all-to-all(f32[8,128,256]{2,1,0:T(8,128)S(1)} %back_and_gram.1), channel_id=1, replica_groups=mesh['y_hi'=2,'x'=4,'y_lo'=2,'z'=4,'core'=2] {'y_hi','x'}, dimensions={0} | all-to-all | bytes 2097152 | tf_op jit(solution)/shard_map/all_to_all | solution.py:451
  156.7 18.7 %all_to_all.22.mine_ref = f32[8,128,256]{2,1,0:T(8,128)S(1)} all-to-all(f32[8,128,256]{2,1,0:T(8,128)S(1)} %add_both.1), channel_id=1, replica_groups=mesh['y_hi'=2,'x'=4,'y_lo'=2,'z'=4,'core'=2] {'y_lo','z'}, dimensions={0} | all-to-all | bytes 2097152 | tf_op jit(solution)/shard_map/all_to_all | solution.py:451
  178.4 30.8 %normalised.1 = (f32[512,256]{1,0:T(8,128)S(1)}, f32[32,512]{1,0:T(8,128)S(1)}, f32[32,512]{1,0:T(8,128)S(1)}) custom-call(s32[5]{0:T(128)S(1)} %stack.57.where_ref, f32[8,128,256]{2,1,0:T(8,128)S(1)} %all_to_all.22.mine_ref, f32[8,128,256]{2,1,0:T(8,128)S(1)} %collective-permute-done.23.other_ref), custom_call_target="tpu_custom_call" | custom-call | flops 26843545600 | bytes 1048576 | tf_op jit(solution)/shard_map/normalised/pallas_call | solution.py:95
  211.8 4.6 %collective-permute-done.25 = f32[32,512]{1,0:T(8,128)S(1)} collective-permute-done((f32[32,512]{1,0:T(8,128)S(1)}, f32[32,512]{1,0:T(8,128)S(1)}, u32[]{:S(2)}, u32[]{:S(2)}) %collective-permute-start.25) | collective-permute-done | bytes 65568 | tf_op jit(solution)/shard_map/ppermute | solution.py:455
  219.5 4.4 %collective-permute-done.28.refs_3_ = f32[2,32,512]{2,1,0:T(8,128)S(1)} collective-permute-done((f32[2,32,512]{2,1,0:T(8,128)S(1)}, f32[2,32,512]{2,1,0:T(8,128)S(1)}, u32[]{:S(2)}, u32[]{:S(2)}) %collective-permute-start.28) | collective-permute-done | bytes 131104 | tf_op jit(solution)/shard_map/ppermute | solution.py:459
  226.5 11.7 %all_to_all.23.mine_ref = f32[8,32,512]{2,1,0:T(8,128)S(1)} all-to-all(f32[8,32,512]{2,1,0:T(8,128)S(1)} %add_in_order.1), channel_id=1, replica_groups=mesh['y_hi'=2,'x'=4,'y_lo'=2,'z'=4,'core'=2] {'y_lo','z'}, dimensions={0} | all-to-all | bytes 1048576 | tf_op jit(solution)/shard_map/all_to_all | solution.py:451
  240.1 17.8 %last_basis.1 = bf16[64,256]{1,0:T(8,128)(2,1)S(1)} custom-call(s32[5]{0:T(128)S(1)} %stack.57.where_ref, f32[8,32,512]{2,1,0:T(8,128)S(1)} %all_to_all.23.mine_ref, f32[8,32,512]{2,1,0:T(8,128)S(1)} %collective-permute-done.29.other_ref, f32[512,256]{1,0:T(8,128)S(1)} %get-tuple-element.36.image_ref), custom_call_target="tpu_custom_call" | custom-call | flops 26843545600 | bytes 1048576 | tf_op jit(solution)/shard_map/last_basis/pallas_call | solution.py:95
  259.1 4.3 %collective-permute-done.30 = bf16[64,256]{1,0:T(8,128)(2,1)S(1)} collective-permute-done((bf16[64,256]{1,0:T(8,128)(2,1)S(1)}, bf16[64,256]{1,0:T(8,128)(2,1)S(1)}, u32[]{:S(2)}, u32[]{:S(2)}) %collective-permute-start.30) | collective-permute-done | bytes 32800 | tf_op jit(solution)/shard_map/ppermute | solution.py:455
  263.5 2.7 collective-permute-start.32
  266.2 3.3 %collective-permute-done.33.refs_3_ = bf16[2,64,256]{2,1,0:T(8,128)(2,1)S(1)} collective-permute-done((bf16[2,64,256]{2,1,0:T(8,128)(2,1)S(1)}, bf16[2,64,256]{2,1,0:T(8,128)(2,1)S(1)}, u32[]{:S(2)}, u32[]{:S(2)}) %collective-permute-start.33) | collective-permute-done | bytes 65568 | tf_op jit(solution)/shard_map/ppermute | solution.py:459
  271.6 3.2 %compress.1 = (f32[32,2048]{1,0:T(8,128)S(1)}, f32[32,2048]{1,0:T(8,128)S(1)}) custom-call(s32[5]{0:T(128)S(1)} %stack.57.where_ref, bf16[2,64,256]{2,1,0:T(8,128)(2,1)S(1)} %pad_maximum_fusion.3.refs_0_, bf16[2,64,256]{2,1,0:T(8,128)(2,1)S(1)} %collective-permute-done.31.refs_1_, bf16[2,64,256]{2,1,0:T(8,128)(2,1)S(1)} %collective-permute-done.32.refs_2_, ...), custom_call_target="tpu_custom_call" | custom-call | flops 4294967296 | bytes 1048576 | tf_op jit(solution)/shard_map/compress/pallas_call | solution.py:95
  (90 shorter events, 71.1 us)
Async XLA Ops:
  0.0 34.9 %collective-permute-start = (bf16[2048,256]{1,0:T(8,128)(2,1)}, bf16[2048,256]{1,0:T(8,128)(2,1)S(1)}, u32[]{:S(2)}, u32[]{:S(2)}) collective-permute-start(bf16[2048,256]{1,0:T(8,128)(2,1)} %x_ref.1), channel_id=1, source_target_pairs={{0,2},{2,4},{4,6},{6,0},{1,3},{3,5},{5,7},{7,1},{8,10},{10,12},{12... | collective-permute-start | bytes 3145736 | tf_op jit(solution)/shard_map/ppermute | solution.py:459
  2.0 32.9 %collective-permute-start.2 = (bf16[2048,256]{1,0:T(8,128)(2,1)}, bf16[2048,256]{1,0:T(8,128)(2,1)S(1)}, u32[]{:S(2)}, u32[]{:S(2)}) collective-permute-start(bf16[2048,256]{1,0:T(8,128)(2,1)} %x_ref.1), channel_id=1, source_target_pairs={{0,8},{8,0},{1,9},{9,1},{2,10},{10,2},{3,11},{11,3},{4,12},{12,4},... | collective-permute-start | bytes 3145736 | tf_op jit(solution)/shard_map/ppermute | solution.py:455
  3.6 31.4 %collective-permute-start.1 = (bf16[2048,256]{1,0:T(8,128)(2,1)}, bf16[2048,256]{1,0:T(8,128)(2,1)S(1)}, u32[]{:S(2)}, u32[]{:S(2)}) collective-permute-start(bf16[2048,256]{1,0:T(8,128)(2,1)} %x_ref.1), channel_id=1, source_target_pairs={{0,6},{2,0},{4,2},{6,4},{1,7},{3,1},{5,3},{7,5},{8,14},{10,8},{12,... | collective-permute-start | bytes 3145736 | tf_op jit(solution)/shard_map/ppermute | solution.py:459
  37.2 23.5 %collective-permute-start.5 = (bf16[2048,256]{1,0:T(8,128)(2,1)}, bf16[2048,256]{1,0:T(8,128)(2,1)S(1)}, u32[]{:S(2)}, u32[]{:S(2)}) collective-permute-start(bf16[2048,256]{1,0:T(8,128)(2,1)} %get-tuple-element.26.refs_4_.refs_8_), channel_id=1, source_target_pairs={{0,6},{2,0},{4,2},{6,4},{1,7},{3,1},{5,3},{7,5},{8,14},{10,8},{12,... | collective-permute-start | bytes 3145736 | tf_op jit(solution)/shard_map/ppermute | solution.py:459
  39.8 24.1 %collective-permute-start.3 = (bf16[2048,256]{1,0:T(8,128)(2,1)}, bf16[2048,256]{1,0:T(8,128)(2,1)S(1)}, u32[]{:S(2)}, u32[]{:S(2)}) collective-permute-start(bf16[2048,256]{1,0:T(8,128)(2,1)} %get-tuple-element.23.refs_1_.refs_5_), channel_id=1, source_target_pairs={{0,2},{2,4},{4,6},{6,0},{1,3},{3,5},{5,7},{7,1},{8,10},{10,12},{12... | collective-permute-start | bytes 3145736 | tf_op jit(solution)/shard_map/ppermute | solution.py:459
  39.8 27.1 %collective-permute-start.4 = (bf16[2048,256]{1,0:T(8,128)(2,1)}, bf16[2048,256]{1,0:T(8,128)(2,1)S(1)}, u32[]{:S(2)}, u32[]{:S(2)}) collective-permute-start(bf16[2048,256]{1,0:T(8,128)(2,1)} %get-tuple-element.23.refs_1_.refs_5_), channel_id=1, source_target_pairs={{0,8},{8,0},{1,9},{9,1},{2,10},{10,2},{3,11},{11,3},{4,12},{12,4},... | collective-permute-start | bytes 3145736 | tf_op jit(solution)/shard_map/ppermute | solution.py:455
  60.8 11.2 %collective-permute-start.7 = (bf16[1024,256]{1,0:T(8,128)(2,1)S(1)}, bf16[1024,256]{1,0:T(8,128)(2,1)S(1)}, u32[]{:S(2)}, u32[]{:S(2)}) collective-permute-start(bf16[1024,256]{1,0:T(8,128)(2,1)S(1)} %slice.12), channel_id=1, source_target_pairs={{0,6},{2,0},{4,2},{6,4},{1,7},{3,1},{5,3},{7,5},{8,14},{10,8},{12,... | collective-permute-start | bytes 1572872 | tf_op jit(solution)/shard_map/ppermute | solution.py:459
  64.6 10.2 %collective-permute-start.6 = (bf16[1024,256]{1,0:T(8,128)(2,1)S(1)}, bf16[1024,256]{1,0:T(8,128)(2,1)S(1)}, u32[]{:S(2)}, u32[]{:S(2)}) collective-permute-start(bf16[1024,256]{1,0:T(8,128)(2,1)S(1)} %get-tuple-element.27), channel_id=1, source_target_pairs={{0,8},{8,0},{1,9},{9,1},{2,10},{10,2},{3,11},{11,3},{4,12},{12,4},... | collective-permute-start | bytes 1572872 | tf_op jit(solution)/shard_map/ppermute | solution.py:455
  82.4 6.8 %collective-permute-start.9 = (f32[2,64,256]{2,1,0:T(8,128)S(1)}, f32[2,64,256]{2,1,0:T(8,128)S(1)}, u32[]{:S(2)}, u32[]{:S(2)}) collective-permute-start(f32[2,64,256]{2,1,0:T(8,128)S(1)} %get-tuple-element.29), channel_id=1, source_target_pairs={{0,16},{16,32},{32,48},{48,0},{1,17},{17,33},{33,49},{49,1},{2,18}... | collective-permute-start | bytes 393224 | tf_op jit(solution)/shard_map/ppermute | solution.py:459
  84.0 7.4 %collective-permute-start.10 = (f32[2,64,256]{2,1,0:T(8,128)S(1)}, f32[2,64,256]{2,1,0:T(8,128)S(1)}, u32[]{:S(2)}, u32[]{:S(2)}) collective-permute-start(f32[2,64,256]{2,1,0:T(8,128)S(1)} %get-tuple-element.30), channel_id=1, source_target_pairs={{0,48},{16,0},{32,16},{48,32},{1,49},{17,1},{33,17},{49,33},{2,50}... | collective-permute-start | bytes 393224 | tf_op jit(solution)/shard_map/ppermute | solution.py:459
  85.7 7.3 %collective-permute-start.11 = (f32[2,64,256]{2,1,0:T(8,128)S(1)}, f32[2,64,256]{2,1,0:T(8,128)S(1)}, u32[]{:S(2)}, u32[]{:S(2)}) collective-permute-start(f32[2,64,256]{2,1,0:T(8,128)S(1)} %get-tuple-element.31), channel_id=1, source_target_pairs={{0,32},{16,48},{32,0},{48,16},{1,33},{17,49},{33,1},{49,17},{2,34}... | collective-permute-start | bytes 393224 | tf_op jit(solution)/shard_map/ppermute | solution.py:459
  93.1 5.8 %collective-permute-start.12 = (f32[64,256]{1,0:T(8,128)S(1)}, f32[64,256]{1,0:T(8,128)S(1)}, u32[]{:S(2)}, u32[]{:S(2)}) collective-permute-start(f32[64,256]{1,0:T(8,128)S(1)} %slice_bitcast_fusion), channel_id=1, source_target_pairs={{0,64},{64,0},{1,65},{65,1},{2,66},{66,2},{3,67},{67,3},{4,68},{68... | collective-permute-start | bytes 196616 | tf_op jit(solution)/shard_map/ppermute | solution.py:455
  105.9 6.6 %collective-permute-start.16 = (f32[2,64,256]{2,1,0:T(8,128)S(1)}, f32[2,64,256]{2,1,0:T(8,128)S(1)}, u32[]{:S(2)}, u32[]{:S(2)}) collective-permute-start(f32[2,64,256]{2,1,0:T(8,128)S(1)} %get-tuple-element.40.refs_0_), channel_id=1, source_target_pairs={{0,32},{16,48},{32,0},{48,16},{1,33},{17,49},{33,1},{49,17},{2,34}... | collective-permute-start | bytes 393224 | tf_op jit(solution)/shard_map/ppermute | solution.py:459
  106.9 6.2 %collective-permute-start.15 = (f32[2,64,256]{2,1,0:T(8,128)S(1)}, f32[2,64,256]{2,1,0:T(8,128)S(1)}, u32[]{:S(2)}, u32[]{:S(2)}) collective-permute-start(f32[2,64,256]{2,1,0:T(8,128)S(1)} %get-tuple-element.40.refs_0_), channel_id=1, source_target_pairs={{0,48},{16,0},{32,16},{48,32},{1,49},{17,1},{33,17},{49,33},{2,50}... | collective-permute-start | bytes 393224 | tf_op jit(solution)/shard_map/ppermute | solution.py:459
  109.8 6.2 %collective-permute-start.14 = (f32[2,64,256]{2,1,0:T(8,128)S(1)}, f32[2,64,256]{2,1,0:T(8,128)S(1)}, u32[]{:S(2)}, u32[]{:S(2)}) collective-permute-start(f32[2,64,256]{2,1,0:T(8,128)S(1)} %get-tuple-element.40.refs_0_), channel_id=1, source_target_pairs={{0,16},{16,32},{32,48},{48,0},{1,17},{17,33},{33,49},{49,1},{2,18}... | collective-permute-start | bytes 393224 | tf_op jit(solution)/shard_map/ppermute | solution.py:459
  119.3 13.1 %collective-permute-start.17 = (f32[64,2048]{1,0:T(8,128)S(1)}, f32[64,2048]{1,0:T(8,128)S(1)}, u32[]{:S(2)}, u32[]{:S(2)}) collective-permute-start(f32[64,2048]{1,0:T(8,128)S(1)} %next_product.1.mine_ref), channel_id=1, source_target_pairs={{0,1},{1,0},{2,3},{3,2},{4,5},{5,4},{6,7},{7,6},{8,9},{9,8},{10,11... | collective-permute-start | bytes 1572872 | tf_op jit(solution)/shard_map/ppermute | solution.py:455
  119.4 8.1 %collective-permute-start.21 = (f32[2,64,256]{2,1,0:T(8,128)S(1)}, f32[2,64,256]{2,1,0:T(8,128)S(1)}, u32[]{:S(2)}, u32[]{:S(2)}) collective-permute-start(f32[2,64,256]{2,1,0:T(8,128)S(1)} %get-tuple-element.39.refs_0_), channel_id=1, source_target_pairs={{0,4},{2,6},{4,0},{6,2},{1,5},{3,7},{5,1},{7,3},{8,12},{10,14},{12... | collective-permute-start | bytes 393224 | tf_op jit(solution)/shard_map/ppermute | solution.py:459
  121.2 7.6 %collective-permute-start.20 = (f32[2,64,256]{2,1,0:T(8,128)S(1)}, f32[2,64,256]{2,1,0:T(8,128)S(1)}, u32[]{:S(2)}, u32[]{:S(2)}) collective-permute-start(f32[2,64,256]{2,1,0:T(8,128)S(1)} %get-tuple-element.39.refs_0_), channel_id=1, source_target_pairs={{0,6},{2,0},{4,2},{6,4},{1,7},{3,1},{5,3},{7,5},{8,14},{10,8},{12,... | collective-permute-start | bytes 393224 | tf_op jit(solution)/shard_map/ppermute | solution.py:459
  122.6 7.3 %collective-permute-start.19 = (f32[2,64,256]{2,1,0:T(8,128)S(1)}, f32[2,64,256]{2,1,0:T(8,128)S(1)}, u32[]{:S(2)}, u32[]{:S(2)}) collective-permute-start(f32[2,64,256]{2,1,0:T(8,128)S(1)} %get-tuple-element.39.refs_0_), channel_id=1, source_target_pairs={{0,2},{2,4},{4,6},{6,0},{1,3},{3,5},{5,7},{7,1},{8,10},{10,12},{12... | collective-permute-start | bytes 393224 | tf_op jit(solution)/shard_map/ppermute | solution.py:459
  216.4 7.6 %collective-permute-start.28 = (f32[2,32,512]{2,1,0:T(8,128)S(1)}, f32[2,32,512]{2,1,0:T(8,128)S(1)}, u32[]{:S(2)}, u32[]{:S(2)}) collective-permute-start(f32[2,32,512]{2,1,0:T(8,128)S(1)} %pad_maximum_fusion.2.refs_0_), channel_id=1, source_target_pairs={{0,32},{16,48},{32,0},{48,16},{1,33},{17,49},{33,1},{49,17},{2,34}... | collective-permute-start | bytes 393224 | tf_op jit(solution)/shard_map/ppermute | solution.py:459
  217.3 6.7 %collective-permute-start.27 = (f32[2,32,512]{2,1,0:T(8,128)S(1)}, f32[2,32,512]{2,1,0:T(8,128)S(1)}, u32[]{:S(2)}, u32[]{:S(2)}) collective-permute-start(f32[2,32,512]{2,1,0:T(8,128)S(1)} %pad_maximum_fusion.2.refs_0_), channel_id=1, source_target_pairs={{0,48},{16,0},{32,16},{48,32},{1,49},{17,1},{33,17},{49,33},{2,50}... | collective-permute-start | bytes 393224 | tf_op jit(solution)/shard_map/ppermute | solution.py:459
  219.5 6.3 %collective-permute-start.26 = (f32[2,32,512]{2,1,0:T(8,128)S(1)}, f32[2,32,512]{2,1,0:T(8,128)S(1)}, u32[]{:S(2)}, u32[]{:S(2)}) collective-permute-start(f32[2,32,512]{2,1,0:T(8,128)S(1)} %pad_maximum_fusion.2.refs_0_), channel_id=1, source_target_pairs={{0,16},{16,32},{32,48},{48,0},{1,17},{17,33},{33,49},{49,1},{2,18}... | collective-permute-start | bytes 393224 | tf_op jit(solution)/shard_map/ppermute | solution.py:459
  263.4 6.1 %collective-permute-start.33 = (bf16[2,64,256]{2,1,0:T(8,128)(2,1)S(1)}, bf16[2,64,256]{2,1,0:T(8,128)(2,1)S(1)}, u32[]{:S(2)}, u32[]{:S(2)}) collective-permute-start(bf16[2,64,256]{2,1,0:T(8,128)(2,1)S(1)} %pad_maximum_fusion.3.refs_0_), channel_id=1, source_target_pairs={{0,32},{16,48},{32,0},{48,16},{1,33},{17,49},{33,1},{49,17},{2,34}... | collective-permute-start | bytes 196616 | tf_op jit(solution)/shard_map/ppermute | solution.py:459
  263.5 6.0 %collective-permute-start.32 = (bf16[2,64,256]{2,1,0:T(8,128)(2,1)S(1)}, bf16[2,64,256]{2,1,0:T(8,128)(2,1)S(1)}, u32[]{:S(2)}, u32[]{:S(2)}) collective-permute-start(bf16[2,64,256]{2,1,0:T(8,128)(2,1)S(1)} %pad_maximum_fusion.3.refs_0_), channel_id=1, source_target_pairs={{0,48},{16,0},{32,16},{48,32},{1,49},{17,1},{33,17},{49,33},{2,50}... | collective-permute-start | bytes 196616 | tf_op jit(solution)/shard_map/ppermute | solution.py:459
  (19 other events, 87.0 us)
